TPU v7x, 32 devices: a whole 2x2x4 slice. The times are simulated.
32 devices in a mesh: dp: 16 (over z, y, x), cuts: 2 (over core).
Axes of the slice: x: 2, y: 2, z: 4, core: 2. Of those that a mesh axis runs over, the one named last changes fastest.
Arguments:
- queries: bfloat16 [128, 2048], P('dp', 'cuts'), may hold values from -240 to 240
- new_keys: bfloat16 [128, 2048], P('dp', 'cuts'), may hold values from -6 to 6
- new_values: bfloat16 [128, 2048], P('dp', 'cuts'), may hold values from -6 to 6
- key_cache: bfloat16 [128, 64, 2048], P('dp', None, 'cuts'), may hold values from -6 to 6
- value_cache: bfloat16 [128, 64, 2048], P('dp', None, 'cuts'), may hold values from -6 to 6
- lengths: int32 [128], P('dp'), may hold values from 1 to 64
- resid: bfloat16 [128, 2048], P('dp'), may hold values from -6 to 6
- norm_gain: float32 [2048], replicated, may hold values from 0.5 to 1.5
- w_out: bfloat16 [2048, 2048], P('cuts'), may hold values from -0.125 to 0.125
- experts: int32 [128, 1], P('dp'), may hold values from 0 to 3; in each aligned block of 8 rows (0 to 7, 8 to 15, ...) at most 4 rows name the same one
- w_up: bfloat16 [16, 2048, 2048], P('dp', None, 'cuts'), may hold values from -0.125 to 0.125
- w_down: bfloat16 [16, 2048, 2048], P('dp', 'cuts'), may hold values from -0.0625 to 0.0625
Outputs:
- mixed: bfloat16 [128, 2048], P('dp', 'cuts')
Inputs may be any that keep to these rules, and one draw needn't show every extreme that they name: `experts`: among the 8 rows of one dp index each expert is named by at most 4 rows, and by exactly 4 in some.
All inputs are finite; a program needn't handle non-finite values.
Results may differ from a plain program's by a relative error of at most 0.014.
Values may be sent and summed in bfloat16 or wider, within the bound.
A program may use at most 64 MiB of HBM per device.

v0:
```python
import jax
import jax.numpy as jnp
from jax import lax
from jax.sharding import PartitionSpec as P

HD = 128
GROUP = 4


def attend_local(queries, new_keys, new_values, key_cache, value_cache, lengths):
    count, feats = queries.shape
    heads = feats // HD
    length = key_cache.shape[1]
    scale = 1.0 / HD**0.5
    query = queries.reshape(count, heads, HD)
    kcache = key_cache.reshape(count, length, heads, HD)
    vcache = value_cache.reshape(count, length, heads, HD)
    nkey = new_keys.reshape(count, heads, HD)
    nval = new_values.reshape(count, heads, HD)
    scores = jnp.einsum("rhd,rjhd->rhj", query, kcache, preferred_element_type=jnp.float32) * scale
    keep = jnp.arange(length)[None, None, :] < lengths[:, None, None]
    scores = jnp.where(keep, scores, -1e30)
    fresh = jnp.einsum("rhd,rhd->rh", query, nkey, preferred_element_type=jnp.float32) * scale
    peak = jnp.maximum(jnp.max(scores, axis=-1), fresh)
    pcache = jnp.where(keep, jnp.exp(scores - peak[..., None]), 0.0)
    pnew = jnp.exp(fresh - peak)
    total = jnp.sum(pcache, axis=-1) + pnew
    pcache = (pcache / total[..., None]).astype(jnp.bfloat16)
    pnew = (pnew / total).astype(jnp.bfloat16)
    summed = jnp.einsum("rhj,rjhd->rhd", pcache, vcache, preferred_element_type=jnp.float32)
    summed = summed + pnew.astype(jnp.float32)[..., None] * nval.astype(jnp.float32)
    return summed.reshape(count, feats).astype(jnp.bfloat16)


def on_device(
    queries,
    new_keys,
    new_values,
    key_cache,
    value_cache,
    lengths,
    resid,
    norm_gain,
    w_out,
    experts,
    w_up,
    w_down,
):
    count = resid.shape[0]
    width_all = resid.shape[1]
    n_cuts = lax.axis_size("cuts")
    n_data = lax.axis_size("dp")
    width = width_all // n_cuts
    cut = lax.axis_index("cuts")
    heads_out = attend_local(queries, new_keys, new_values, key_cache, value_cache, lengths)
    partial_attn = jnp.dot(heads_out, w_out, preferred_element_type=jnp.float32)
    gain_cols = lax.dynamic_slice_in_dim(norm_gain, cut * width, width, 0)
    attn = lax.psum(partial_attn, "cuts")
    hidden = resid.astype(jnp.float32) + attn
    meansq = jnp.mean(hidden * hidden, axis=-1)
    hidden_cols = lax.dynamic_slice_in_dim(hidden, cut * width, width, 1)
    normed_cols = (hidden_cols * lax.rsqrt(meansq + 1e-06)[:, None] * gain_cols[None, :]).astype(
        jnp.bfloat16
    )
    n_experts = n_data // GROUP
    slots = max(2, 2 * count * GROUP // n_data)
    ids = experts[:, 0]
    order_idx = jnp.arange(count, dtype=jnp.int32)
    earlier = (ids[:, None] == ids[None, :]) & (order_idx[:, None] > order_idx[None, :])
    slot = jnp.sum(earlier.astype(jnp.int32), axis=1)
    slot_id = ids * slots + slot
    table = jnp.arange(n_experts * slots, dtype=jnp.int32)[:, None] == slot_id[None, :]
    full_rows = lax.all_gather(normed_cols, "cuts", axis=1, tiled=True)
    packed = jnp.dot(
        table.astype(jnp.bfloat16), full_rows, preferred_element_type=jnp.float32
    ).astype(jnp.bfloat16)
    packed = packed.reshape(n_experts, slots, full_rows.shape[1])
    received = lax.all_to_all(
        jnp.repeat(packed, GROUP, axis=0), "dp", split_axis=0, concat_axis=0, tiled=True
    )
    arrived = received.reshape(n_data * slots, width_all)
    act = jax.nn.gelu(jnp.dot(arrived, w_up[0], preferred_element_type=jnp.float32)).astype(
        jnp.bfloat16
    )
    lower = w_down[0]
    share = lax.psum_scatter(
        lax.dot_general(
            lower, act, (((0,), (1,)), ((), ())), preferred_element_type=jnp.float32
        ).astype(jnp.bfloat16),
        "cuts",
        scatter_dimension=0,
        tiled=True,
    )
    outgoing = share.reshape(width, n_data, slots)
    returned = lax.all_to_all(outgoing, "dp", split_axis=1, concat_axis=1, tiled=True)
    grouped = returned.astype(jnp.float32).reshape(width, n_experts, GROUP, slots)
    combined = jnp.sum(grouped, axis=2).reshape(width, n_experts * slots)
    expert_cols = jnp.einsum(
        "ck,kr->rc", combined, table.astype(jnp.float32), precision=lax.Precision.HIGHEST
    )
    return (hidden_cols + expert_cols).astype(jnp.bfloat16)


def solution(mesh):
    placed = (
        P("dp", "cuts"),
        P("dp", "cuts"),
        P("dp", "cuts"),
        P("dp", None, "cuts"),
        P("dp", None, "cuts"),
        P("dp"),
        P("dp", None),
        P(),
        P("cuts", None),
        P("dp", None),
        P("dp", None, "cuts"),
        P("dp", "cuts", None),
    )
    return jax.shard_map(
        on_device, mesh=mesh, in_specs=placed, out_specs=P("dp", "cuts"), check_vma=False
    )
```

profile of v0, /device:TPU:0, one launch (start us, length us, event | category | flops | bytes accessed | tf_op | source)
XLA Modules:
  0.0 90.1 jit_solution(17500733721410618997)
XLA Ops:
  6.5 0.0 copy-start
  6.5 0.0 all-reduce.2.cloned.1.call-start
  6.6 0.8 iota_compare_fusion.4
  7.4 0.8 fusion.37
  8.2 0.1 copy.24
  8.3 1.9 %fusion.14 = f32[8,8,1,64]{3,2,1,0:T(1,128)S(1)} fusion(bf16[8,8,128,1]{2,0,1,3:T(8,128)(2,1)} %bitcast.74, bf16[8,64,1024]{2,1,0:T(8,128)(2,1)} %param.15), kind=kOutput, calls=%fused_computation.12 | convolution fusion | flops 1048576 | bytes 1081344 | tf_op jit(solution)/shard_map/rhd,rjhd->rhj/dot_general | solution.py:20
  10.2 0.1 fusion.40
  10.3 0.2 fusion.41
  10.5 0.1 fusion.47
  10.6 0.1 copy.17
  10.6 0.0 copy-done
  10.6 0.4 fusion.11
  11.0 3.5 %fusion.43 = f32[8,2048]{1,0:T(8,128)} fusion(bf16[1024,2048]{1,0:T(8,128)(2,1)} %param.20, f32[8,8,1,128]{3,2,1,0:T(1,128)S(1)} %fusion.11, bf16[8,1024]{1,0:T(8,128)(2,1)} %param.14, f32[8,8]{0,1:T(8,128)S(1)} %copy.17), kind=kOutput, calls=%fused_computation.45 | convolution fusion | flops 33587200 | bytes 4309248 | tf_op jit(solution)/shard_map/dot_general | solution.py:56
  14.5 0.0 all-reduce.2.cloned.1.call-update
  14.6 0.0 reduce-scatter.2.cloned.1.call-start
  14.6 0.2 convert_reduce_fusion.1
  14.8 20.3 %all-reduce.2.cloned.1.call-done = f32[8,2048]{1,0:T(8,128)} async-done(((f32[8,2048]{1,0:T(8,128)}), f32[8,2048]{1,0:T(8,128)}) %all-reduce.2.cloned.1.call-update) | async-done | bytes 65552 | tf_op jit(solution)/shard_map/psum | solution.py:58
  35.1 0.0 copy-done.1
  35.1 1.0 %multiply_reduce_fusion = (f32[8]{0:T(128)S(1)}, f32[8,2048]{1,0:T(8,128)S(1)}) fusion(f32[8,2048]{1,0:T(8,128)} %all-reduce.2.cloned.1.call-done, bf16[8,2048]{1,0:T(8,128)(2,1)S(1)} %copy-done.1), kind=kLoop, calls=%fused_computation.29 | loop fusion | flops 65528 | bytes 163872 | tf_op jit(solution)/shard_map/reduce_sum | solution.py:60
  36.1 0.1 multiply_convert_fusion
  36.2 1.8 %all_gather.3 = bf16[8,2048]{1,0:T(8,128)(2,1)S(1)} all-gather(bf16[8,1024]{1,0:T(8,128)(2,1)S(1)} %multiply_convert_fusion), channel_id=1, replica_groups=mesh['dp'=16,'cuts'=2] {'cuts'}, dimensions={1}, use_global_device_ids=true | all-gather | bytes 49152 | tf_op jit(solution)/shard_map/all_gather | solution.py:73
  38.0 0.1 convolution_convert_fusion
  38.2 0.1 broadcast_in_dim.35
  38.3 16.9 %all_to_all.10 = bf16[16,4,2048]{2,1,0:T(4,128)(2,1)S(1)} all-to-all(bf16[16,4,2048]{2,1,0:T(4,128)(2,1)S(1)} %bitcast.70), channel_id=1, replica_groups=mesh['dp'=16,'cuts'=2] {'dp'}, dimensions={0} | all-to-all | bytes 524288 | tf_op jit(solution)/shard_map/all_to_all | solution.py:78
  55.2 0.1 reshape.83
  55.3 5.8 %fusion.7 = bf16[2048,64]{0,1:T(8,128)(2,1)} fusion(bf16[1,1024,2048]{2,1,0:T(8,128)(2,1)} %param.23, bf16[64,2048]{1,0:T(8,128)(2,1)S(1)} %reshape.83, bf16[1,2048,1024]{2,1,0:T(8,128)(2,1)} %param.22), kind=kOutput, calls=%fused_computation.5 | convolution fusion | flops 537591808 | bytes 8912896 | tf_op jit(solution)/shard_map/dot_general | solution.py:87
  61.1 0.0 reduce-scatter.2.cloned.1.call-update
  61.1 5.7 %reduce-scatter.2.cloned.1.call-done = bf16[1024,64]{0,1:T(8,128)(2,1)} async-done(((bf16[2048,64]{0,1:T(8,128)(2,1)}), bf16[1024,64]{0,1:T(8,128)(2,1)}) %reduce-scatter.2.cloned.1.call-update) | async-done | bytes 131088 | tf_op jit(solution)/shard_map/reduce_scatter | solution.py:86
  66.8 1.0 %reshape.84 = bf16[1024,16,4]{0,2,1:T(4,128)(2,1)S(1)} reshape(bf16[1024,64]{0,1:T(8,128)(2,1)} %reduce-scatter.2.cloned.1.call-done) | data formatting | bytes 262144 | tf_op jit(solution)/shard_map/reshape | solution.py:94
  67.8 14.5 %all_to_all.11 = bf16[1024,16,4]{0,2,1:T(4,128)(2,1)S(1)} all-to-all(bf16[1024,16,4]{0,2,1:T(4,128)(2,1)S(1)} %reshape.84), channel_id=1, replica_groups=mesh['dp'=16,'cuts'=2] {'dp'}, dimensions={1} | all-to-all | bytes 262144 | tf_op jit(solution)/shard_map/all_to_all | solution.py:95
  82.3 0.1 convert_reduce_fusion
  82.4 0.8 fusion.10
  (12 shorter events, 0.1 us)
Async XLA Ops:
  6.5 4.1 %copy-start = (bf16[8,64,1024]{2,1,0:T(8,128)(2,1)S(1)}, bf16[8,64,1024]{2,1,0:T(8,128)(2,1)}, u32[]{:S(2)}) copy-start(bf16[8,64,1024]{2,1,0:T(8,128)(2,1)} %param.16) | copy-start | bytes 3145732
  6.5 8.1 %copy-start.3 = (s32[8,1]{0,1:T(1,128)S(1)}, s32[8,1]{0,1:T(1,128)}, u32[]{:S(2)}) copy-start(s32[8,1]{0,1:T(1,128)} %param.21) | copy-start | bytes 100
  6.5 8.3 %copy-start.2 = (f32[2048]{0:T(1024)S(1)}, f32[2048]{0:T(1024)}, u32[]{:S(2)}) copy-start(f32[2048]{0:T(1024)} %param.19) | copy-start | bytes 24580
  6.5 28.6 %copy-start.1 = (bf16[8,2048]{1,0:T(8,128)(2,1)S(1)}, bf16[8,2048]{1,0:T(8,128)(2,1)}, u32[]{:S(2)}) copy-start(bf16[8,2048]{1,0:T(8,128)(2,1)} %param.18) | copy-start | bytes 98308
  6.5 28.6 %all-reduce.2.cloned.1.call-start = ((), (), s32[]{:S(2)}) async-start(), calls=%async_computation.3 | async-start | bytes 131072 | tf_op jit(solution)/shard_map/psum | solution.py:58
  14.6 52.3 %reduce-scatter.2.cloned.1.call-start = ((), (), s32[]{:S(2)}) async-start(), calls=%async_computation.4 | async-start | bytes 393216 | tf_op jit(solution)/shard_map/reduce_scatter | solution.py:86
Sparse Core Ops, SparseCore 0:
  14.7 20.3 all-reduce.1
  61.2 5.5 reduce-scatter.1
where the time goes:
time: 90.6 us; the launch traced here: 90.1 us
  blocking collectives  33.2 us (37%)
  waiting for transfers between devices  26 us (29%)
  between operations  13.5 us (15%)
  matrix products  12.5 us (14%)
  other arithmetic  3.32 us (4%)
  local copies, waits for them, and re-layouts  1.35 us (1%)
    psum x1, waiting for transfers between devices, on_device(): attn = lax.psum(partial_attn, 'cuts')  20.3 us
    all_to_all x1, blocking collectives, on_device(): lax.all_to_all(jnp.repeat(packed, GROUP, axis=0), 'dp', split_axis=0, con...  16.9 us
    all_to_all x1, blocking collectives, on_device(): lax.all_to_all(outgoing, 'dp', split_axis=1, concat_axis=1, tiled=True)  14.5 us
    dot_general x1, matrix products, on_device(): lax.dot_general(lower, act, (((0,), (1,)), ((), ())), preferred_element_t...  5.8 us
    reduce_scatter x1, waiting for transfers between devices, on_device(): lax.psum_scatter(lax.dot_general(lower, act, (((0,), (1,)), ((), ())), pr...  5.74 us
    dot_general x1, matrix products, on_device(): partial_attn = jnp.dot(heads_out, w_out, preferred_element_type=jnp.float32)  3.53 us
    dot_general x1, matrix products, attend_local(): jnp.einsum('rhd,rjhd->rhj', query, kcache, preferred_element_type=jnp.flo...  1.88 us
    all_gather x1, blocking collectives, on_device(): full_rows = lax.all_gather(normed_cols, 'cuts', axis=1, tiled=True)  1.82 us
  transfers between devices with their start and end apart: 2, of which 2 were waited for; matrix products, arithmetic and copies ran while one was open for 0% of the time, Pallas kernels for 0%

commit v1 on v0

v1 whole, which is shorter than its diff:
```python
import functools

import jax
import jax.numpy as jnp
from jax import lax
from jax.experimental import pallas as pl
from jax.experimental.pallas import tpu as pltpu
from jax.sharding import PartitionSpec as P

HD = 128
GROUP = 4
TILE = 16
MESH = pl.DeviceIdType.MESH
F32 = jnp.float32
BF16 = jnp.bfloat16


def iota(shape, dim):
    return lax.broadcasted_iota(jnp.int32, shape, dim)


def div(x, n):
    return x >> (n.bit_length() - 1)


def mod(x, n):
    return x & (n - 1)


def one_hot(flags):
    return jnp.where(flags, 1.0, 0.0).astype(BF16)


def mm(a, b):
    return jnp.dot(a, b, preferred_element_type=F32)


def kernel(
    n_data,
    n_cuts,
    lengths,
    experts,
    q_hbm,
    nk_hbm,
    nv_hbm,
    k_hbm,
    v_hbm,
    resid_hbm,
    gain_hbm,
    wout_hbm,
    wup_hbm,
    wdown_hbm,
    out_ref,
    q_ref,
    nk_ref,
    nv_ref,
    k_ref,
    v_ref,
    resid_ref,
    gain_ref,
    wout_ref,
    wup_ref,
    wdown_ref,
    parts,
    hid_ref,
    packed,
    gath,
    mine,
    halves,
    share,
    red,
    going,
    back,
    load_sem,
    part_send,
    part_recv,
    z_send,
    z_recv,
    spread_send,
    spread_recv,
    half_send,
    half_recv,
    red_send,
    red_recv,
    back_send,
    back_recv,
):
    dp = lax.axis_index("dp")
    cut = lax.axis_index("cuts")
    me = dp // GROUP
    g = lax.rem(dp, GROUP)
    n_e = n_data // GROUP
    count, feats = q_ref.shape
    width_all = resid_ref.shape[1]
    width = width_all // n_cuts
    heads = feats // HD
    length = k_hbm.shape[1]
    slots = max(2, 2 * count * GROUP // n_data)
    scale = 1.0 / HD**0.5

    loads = [
        pltpu.make_async_copy(src, dst, load_sem.at[i])
        for i, (src, dst) in enumerate(
            (
                (q_hbm, q_ref),
                (nk_hbm, nk_ref),
                (k_hbm, k_ref),
                (nv_hbm, nv_ref),
                (v_hbm, v_ref),
                (resid_hbm, resid_ref),
                (gain_hbm, gain_ref),
                (wout_hbm, wout_ref),
                (wup_hbm.at[0], wup_ref),
                (wdown_hbm.at[0], wdown_ref),
            )
        )
    ]
    for load in loads:
        load.start()

    cut_peers = [lax.rem(cut + d, n_cuts) for d in range(1, n_cuts)]
    e_peers = [lax.rem(me + d, n_e) for d in range(1, n_e)]
    g_peers = [lax.rem(g + d, GROUP) for d in range(1, GROUP)]
    ids = [(dp, c) for c in cut_peers]
    ids += [(e * GROUP + g, cut) for e in e_peers]
    ids += [(me * GROUP + h, cut) for h in g_peers]
    barrier = pltpu.get_barrier_semaphore()
    for device in ids:
        pl.semaphore_signal(barrier, inc=1, device_id=device, device_id_type=MESH)

    def remote(src, dst, send, recv, device):
        return pltpu.make_async_remote_copy(
            src_ref=src, dst_ref=dst, send_sem=send, recv_sem=recv, device_id=device, device_id_type=MESH
        )

    sent = []

    pairs = count * heads
    spread_rows = one_hot(div(iota((pairs, count), 0), heads) == iota((pairs, count), 1))
    own_head = div(iota((pairs, feats), 1), HD) == mod(iota((pairs, feats), 0), heads)
    loads[0].wait()
    q_wide = jnp.where(own_head, mm(spread_rows, q_ref[...]), 0.0).astype(BF16)
    nt = (((1,), (1,)), ((), ()))
    loads[1].wait()
    fresh_all = lax.dot_general(q_wide, nk_ref[...], nt, preferred_element_type=F32)
    own_new = div(iota((pairs, count), 0), heads) == iota((pairs, count), 1)
    fresh = jnp.sum(jnp.where(own_new, fresh_all, 0.0), axis=1, keepdims=True) * scale
    loads[2].wait()
    span = count * length
    keys = k_ref[...].reshape(span, feats)
    scores = lax.dot_general(q_wide, keys, nt, preferred_element_type=F32) * scale
    col = iota((1, span), 1)
    limit = jnp.zeros((1, span), jnp.int32)
    for t in range(count):
        limit = jnp.where(div(col, length) == t, lengths[t], limit)
    valid = jnp.where(mod(col, length) < limit, div(col, length), -1)
    keep = div(iota((pairs, span), 0), heads) == valid
    scores = jnp.where(keep, scores, -1e30)
    peak = jnp.maximum(jnp.max(scores, axis=1, keepdims=True), fresh)
    pcache = jnp.where(keep, jnp.exp(scores - peak), 0.0)
    pnew = jnp.exp(fresh - peak)
    total = jnp.sum(pcache, axis=1, keepdims=True) + pnew
    pcache = (pcache / total).astype(BF16)
    pnew = (pnew / total).astype(BF16).astype(F32)
    loads[3].wait()
    new_rows = mm(spread_rows, nv_ref[...])
    loads[4].wait()
    summed = mm(pcache, v_ref[...].reshape(span, feats)) + pnew * new_rows
    summed = jnp.where(own_head, summed, 0.0).astype(BF16)
    join_rows = one_hot(div(iota((count, pairs), 1), heads) == iota((count, pairs), 0))
    heads_out = mm(join_rows, summed).astype(BF16)

    loads[7].wait()
    parts[cut] = mm(heads_out, wout_ref[...])
    pl.semaphore_wait(barrier, len(ids))
    for i, c in enumerate(cut_peers):
        copy = remote(parts.at[cut], parts.at[cut], part_send.at[i], part_recv.at[cut], (dp, c))
        copy.start()
        sent.append(copy)

    ids_of = [experts[t] for t in range(count)]
    place = []
    for t in range(count):
        slot = jnp.int32(0)
        for u in range(t):
            slot = slot + jnp.where(ids_of[u] == ids_of[t], 1, 0)
        place.append(ids_of[t] * slots + slot)
    nk = TILE // slots
    chunk = width_all // nk
    table_shape = (n_e * TILE, nk * count)
    row, col = iota(table_shape, 0), iota(table_shape, 1)
    target = jnp.zeros(table_shape, jnp.int32)
    for t in range(count):
        target = jnp.where(mod(col, count) == t, place[t], target)
    pack = one_hot(
        (div(mod(row, TILE), slots) == div(col, count))
        & (div(row, TILE) * slots + mod(row, slots) == target)
    )
    loads[5].wait()
    loads[6].wait()
    for c in cut_peers:
        remote(parts.at[c], parts.at[c], part_send.at[0], part_recv.at[c], (dp, c)).wait_recv()
    attn = parts[0]
    for c in range(1, n_cuts):
        attn = attn + parts[c]
    hidden = resid_ref[...].astype(F32) + attn
    hid_ref[...] = hidden
    meansq = jnp.mean(hidden * hidden, axis=1, keepdims=True)
    normed = hidden * lax.rsqrt(meansq + 1e-06) * gain_ref[...]
    stacked = jnp.concatenate([normed[:, k * chunk : (k + 1) * chunk] for k in range(nk)], axis=0)
    rows = mm(pack, stacked.astype(BF16)).astype(BF16)
    packed[...] = rows.reshape(n_e, TILE, chunk)

    for i, e in enumerate(e_peers):
        copy = remote(
            packed.at[e], gath.at[g, me], z_send.at[i], z_recv.at[me], (e * GROUP + g, cut)
        )
        copy.start()
        sent.append(copy)
    gath[g, me] = packed[me]
    for i, e in enumerate([me] + e_peers):
        if i > 0:
            remote(
                packed.at[e], gath.at[g, e], z_send.at[i - 1], z_recv.at[e], (e * GROUP + g, cut)
            ).wait_recv()
        for j, h in enumerate(g_peers):
            copy = remote(
                gath.at[g, e],
                gath.at[g, e],
                spread_send.at[j, i],
                spread_recv.at[g, e],
                (me * GROUP + h, cut),
            )
            copy.start()
            sent.append(copy)
    all_rows = GROUP * n_e * slots
    per_group = n_e * slots
    wide = GROUP * n_e * TILE
    row, col = iota((nk * all_rows, wide), 0), iota((nk * all_rows, wide), 1)
    which, m = div(row, all_rows), mod(row, all_rows)
    unpack = one_hot(col == div(m, slots) * TILE + which * slots + mod(m, slots))
    for i, e in enumerate([me] + e_peers):
        for j, h in enumerate(g_peers):
            remote(
                gath.at[h, e],
                gath.at[h, e],
                spread_send.at[j, i],
                spread_recv.at[h, e],
                (me * GROUP + h, cut),
            ).wait_recv()
    arrived = mm(unpack, gath[...].reshape(wide, chunk)).astype(BF16)
    loads[8].wait()
    up = mm(arrived[0:all_rows], wup_ref[0:chunk, :])
    for k in range(1, nk):
        up = up + mm(
            arrived[k * all_rows : (k + 1) * all_rows], wup_ref[k * chunk : (k + 1) * chunk, :]
        )
    act = jax.nn.gelu(up).astype(BF16)

    loads[9].wait()
    for i, c in enumerate(cut_peers + [cut]):
        columns = pl.ds(pl.multiple_of(c * width, width), width)
        mine[c] = mm(act, wdown_ref[:, columns]).astype(BF16)
        if i < n_cuts - 1:
            copy = remote(mine.at[c], halves.at[cut], half_send.at[i], half_recv.at[cut], (dp, c))
            copy.start()
            sent.append(copy)
    summed = mine[cut].astype(F32)
    for i, c in enumerate(cut_peers):
        remote(mine.at[c], halves.at[c], half_send.at[i], half_recv.at[c], (dp, c)).wait_recv()
        summed = summed + halves[c].astype(F32)
    share[...] = summed.astype(BF16).reshape(GROUP, per_group, width)

    for j, h in enumerate(g_peers):
        copy = remote(share.at[h], red.at[g], red_send.at[j], red_recv.at[g], (me * GROUP + h, cut))
        copy.start()
        sent.append(copy)
    nq = min(TILE // slots, width // 128)
    piece = width // nq
    row, col = iota((n_e * TILE, nq * per_group), 0), iota((n_e * TILE, nq * per_group), 1)
    repack = one_hot(
        (div(mod(row, TILE), slots) == div(col, per_group))
        & (div(row, TILE) * slots + mod(row, slots) == mod(col, per_group))
    )
    summed = share[g].astype(F32)
    for j, h in enumerate(g_peers):
        remote(share.at[h], red.at[h], red_send.at[j], red_recv.at[h], (me * GROUP + h, cut)).wait_recv()
        summed = summed + red[h].astype(F32)
    stacked = jnp.concatenate([summed[:, k * piece : (k + 1) * piece] for k in range(nq)], axis=0)
    going[...] = mm(repack, stacked.astype(BF16)).astype(BF16).reshape(n_e, TILE, piece)

    for i, e in enumerate(e_peers):
        copy = remote(
            going.at[e], back.at[me], back_send.at[i], back_recv.at[me], (e * GROUP + g, cut)
        )
        copy.start()
        sent.append(copy)
    back[me] = going[me]
    table_shape = (count, n_e * TILE)
    row, col = iota(table_shape, 0), iota(table_shape, 1)
    target = jnp.zeros(table_shape, jnp.int32)
    for t in range(count):
        target = jnp.where(row == t, place[t], target)
    found = div(col, TILE) * slots + mod(col, slots) == target
    picks = [one_hot(found & (div(mod(col, TILE), slots) == k)) for k in range(nq)]
    for i, e in enumerate(e_peers):
        remote(
            going.at[e], back.at[e], back_send.at[i], back_recv.at[e], (e * GROUP + g, cut)
        ).wait_recv()
    returned = back[...].reshape(n_e * TILE, piece)
    expert_cols = jnp.concatenate([mm(pick, returned) for pick in picks], axis=1)
    hidden_cols = hid_ref[:, pl.ds(pl.multiple_of(cut * width, width), width)]
    out_ref[...] = (hidden_cols + expert_cols).astype(BF16)
    for copy in sent:
        copy.wait_send()


def on_device(
    n_data,
    n_cuts,
    queries,
    new_keys,
    new_values,
    key_cache,
    value_cache,
    lengths,
    resid,
    norm_gain,
    w_out,
    experts,
    w_up,
    w_down,
):
    count, feats = queries.shape
    width_all = resid.shape[1]
    width = width_all // n_cuts
    n_e = n_data // GROUP
    slots = max(2, 2 * count * GROUP // n_data)
    chunk = width_all * slots // TILE
    piece = width // min(TILE // slots, width // 128)
    per_group = n_e * slots
    all_rows = GROUP * per_group
    dma = pltpu.SemaphoreType.DMA
    smem = pl.BlockSpec(memory_space=pltpu.SMEM)
    hbm = pl.BlockSpec(memory_space=pl.ANY)
    return pl.pallas_call(
        functools.partial(kernel, n_data, n_cuts),
        out_shape=jax.ShapeDtypeStruct((count, width), BF16),
        in_specs=[smem, smem] + [hbm] * 10,
        out_specs=pl.BlockSpec(memory_space=pltpu.VMEM),
        scratch_shapes=[
            pltpu.VMEM(queries.shape, BF16),
            pltpu.VMEM(new_keys.shape, BF16),
            pltpu.VMEM(new_values.shape, BF16),
            pltpu.VMEM(key_cache.shape, BF16),
            pltpu.VMEM(value_cache.shape, BF16),
            pltpu.VMEM(resid.shape, BF16),
            pltpu.VMEM((1, width_all), F32),
            pltpu.VMEM(w_out.shape, BF16),
            pltpu.VMEM(w_up.shape[1:], BF16),
            pltpu.VMEM(w_down.shape[1:], BF16),
            pltpu.VMEM((n_cuts, count, width_all), F32),
            pltpu.VMEM((count, width_all), F32),
            pltpu.VMEM((n_e, TILE, chunk), BF16),
            pltpu.VMEM((GROUP, n_e, TILE, chunk), BF16),
            pltpu.VMEM((n_cuts, all_rows, width), BF16),
            pltpu.VMEM((n_cuts, all_rows, width), BF16),
            pltpu.VMEM((GROUP, per_group, width), BF16),
            pltpu.VMEM((GROUP, per_group, width), BF16),
            pltpu.VMEM((n_e, TILE, piece), BF16),
            pltpu.VMEM((n_e, TILE, piece), BF16),
            dma((10,)),
            dma((n_cuts,)),
            dma((n_cuts,)),
            dma((n_e,)),
            dma((n_e,)),
            dma((GROUP, n_e)),
            dma((GROUP, n_e)),
            dma((n_cuts,)),
            dma((n_cuts,)),
            dma((GROUP,)),
            dma((GROUP,)),
            dma((n_e,)),
            dma((n_e,)),
        ],
        compiler_params=pltpu.CompilerParams(
            collective_id=0, has_side_effects=True, vmem_limit_bytes=48 * 1024 * 1024
        ),
    )(
        lengths,
        experts.reshape(count),
        queries,
        new_keys,
        new_values,
        key_cache,
        value_cache,
        resid,
        norm_gain.reshape(1, width_all),
        w_out,
        w_up,
        w_down,
    )


def solution(mesh):
    placed = (
        P("dp", "cuts"),
        P("dp", "cuts"),
        P("dp", "cuts"),
        P("dp", None, "cuts"),
        P("dp", None, "cuts"),
        P("dp"),
        P("dp", None),
        P(),
        P("cuts", None),
        P("dp", None),
        P("dp", None, "cuts"),
        P("dp", "cuts", None),
    )
    return jax.shard_map(
        functools.partial(on_device, mesh.shape["dp"], mesh.shape["cuts"]),
        mesh=mesh,
        in_specs=placed,
        out_specs=P("dp", "cuts"),
        check_vma=False,
    )
```

time: 90.6 us -> 34.9 us (0.39)
  blocking collectives: 33.2 us -> 0 us
  Pallas kernels: 0 us -> 26.4 us
  waiting for transfers between devices: 26 us -> 0 us
  between operations: 13.5 us -> 0.02 us
  matrix products: 12.5 us -> 0 us
  local copies, waits for them, and re-layouts: 1.35 us -> 7.97 us
  other arithmetic: 3.32 us -> 0 us
    all_to_all x2 -> x0, blocking collectives: 31.4 us -> none  [the longest x1 16.9 us: on_device(): lax.all_to_all(jnp.repeat(packed, GROUP, axis=0), 'dp', split_axis=0, con...]
    pallas_call x0 -> x1, Pallas kernels: none -> 26.4 us  [on_device(): pl.pallas_call(functools.partial(kernel, n_data, n_cuts), out_shape=jax.S...]
    psum x1 -> x0, waiting for transfers between devices: 20.3 us -> none  [on_device(): attn = lax.psum(partial_attn, 'cuts')]
    dot_general x6 -> x0, matrix products: 12.5 us -> none  [the longest x1 5.8 us: on_device(): lax.dot_general(lower, act, (((0,), (1,)), ((), ())), preferred_element_t...]
    unnamed x8 -> x19, local copies, waits for them, and re-layouts: 0.02 us -> 7.97 us
    reduce_scatter x1 -> x0, waiting for transfers between devices: 5.74 us -> none  [on_device(): lax.psum_scatter(lax.dot_general(lower, act, (((0,), (1,)), ((), ())), pr...]
    all_gather x1 -> x0, blocking collectives: 1.82 us -> none  [on_device(): full_rows = lax.all_gather(normed_cols, 'cuts', axis=1, tiled=True)]
    reduce_sum x4 -> x0, other arithmetic: 1.38 us -> none  [the longest x1 0.97 us: on_device(): meansq = jnp.mean(hidden * hidden, axis=-1)]
  transfers between devices with their start and end apart: 2 -> 0, of which waited for: 2 -> 0; matrix products, arithmetic and copies ran while one was open for 0% -> 0% of each run, Pallas kernels for 0% -> 0%
where the time goes in v1:
time: 34.9 us; the launch traced here: 34.4 us
  Pallas kernels  26.4 us (76%)
  local copies, waits for them, and re-layouts  7.97 us (23%)
    pallas_call x1, Pallas kernels, on_device(): pl.pallas_call(functools.partial(kernel, n_data, n_cuts), out_shape=jax.S...  26.4 us
    unnamed x19, local copies, waits for them, and re-layouts  7.97 us

profile of v1, /device:TPU:0, one launch (start us, length us, event | category | flops | bytes accessed | tf_op | source)
XLA Modules:
  0.0 34.4 jit_solution(4424976003272290792)
XLA Ops:
  0.0 0.0 copy-start
  0.0 1.2 %copy-done = bf16[8,64,1024]{2,1,0:T(8,128)(2,1)S(1)} copy-done((bf16[8,64,1024]{2,1,0:T(8,128)(2,1)S(1)}, bf16[8,64,1024]{2,1,0:T(8,128)(2,1)}, u32[]{:S(2)}) %copy-start) | copy-done | bytes 1048600
  1.2 0.0 copy-start.1
  1.2 1.2 %copy-done.1 = bf16[8,64,1024]{2,1,0:T(8,128)(2,1)S(1)} copy-done((bf16[8,64,1024]{2,1,0:T(8,128)(2,1)S(1)}, bf16[8,64,1024]{2,1,0:T(8,128)(2,1)}, u32[]{:S(2)}) %copy-start.1) | copy-done | bytes 1048600
  2.5 0.0 copy-start.2
  2.5 0.8 %copy-done.2 = bf16[8,2048]{1,0:T(8,128)(2,1)S(1)} copy-done((bf16[8,2048]{1,0:T(8,128)(2,1)S(1)}, bf16[8,2048]{1,0:T(8,128)(2,1)}, u32[]{:S(2)}) %copy-start.2) | copy-done | bytes 32792
  3.2 0.0 copy-start.3
  3.2 0.7 %copy-done.3 = bf16[8,1024]{1,0:T(8,128)(2,1)S(1)} copy-done((bf16[8,1024]{1,0:T(8,128)(2,1)S(1)}, bf16[8,1024]{1,0:T(8,128)(2,1)}, u32[]{:S(2)}) %copy-start.3) | copy-done | bytes 16408
  3.9 0.0 copy-start.4
  3.9 0.7 %copy-done.4 = bf16[8,1024]{1,0:T(8,128)(2,1)S(1)} copy-done((bf16[8,1024]{1,0:T(8,128)(2,1)S(1)}, bf16[8,1024]{1,0:T(8,128)(2,1)}, u32[]{:S(2)}) %copy-start.4) | copy-done | bytes 16408
  4.6 0.0 copy-start.5
  4.6 0.7 %copy-done.5 = bf16[8,1024]{1,0:T(8,128)(2,1)S(1)} copy-done((bf16[8,1024]{1,0:T(8,128)(2,1)S(1)}, bf16[8,1024]{1,0:T(8,128)(2,1)}, u32[]{:S(2)}) %copy-start.5) | copy-done | bytes 16408
  5.4 0.0 copy-start.6
  5.4 0.7 %copy-done.6 = f32[2048]{0:T(1024)S(1)} copy-done((f32[2048]{0:T(1024)S(1)}, f32[2048]{0:T(1024)}, u32[]{:S(2)}) %copy-start.6) | copy-done | bytes 8216
  6.1 0.0 copy-start.7
  6.1 0.7 %copy-done.7 = s32[8]{0:T(128)S(1)} copy-done((s32[8]{0:T(128)S(1)}, s32[8]{0:T(128)}, u32[]{:S(2)}) %copy-start.7) | copy-done | bytes 56
  6.7 0.0 copy-start.8
  6.7 0.7 %copy-done.8 = s32[8,1]{0,1:T(1,128)S(1)} copy-done((s32[8,1]{0,1:T(1,128)S(1)}, s32[8,1]{0,1:T(1,128)}, u32[]{:S(2)}) %copy-start.8) | copy-done | bytes 56
  7.4 26.4 %shard_map.118 = bf16[8,1024]{1,0:T(8,128)(2,1)S(1)} custom-call(s32[8]{0:T(128)S(1)} %copy-done.7, s32[8]{0:T(128)S(1)} %bitcast.3, bf16[8,1024]{1,0:T(8,128)(2,1)S(1)} %copy-done.3, bf16[8,1024]{1,0:T(8,128)(2,1)S(1)} %copy-done.4, bf16[8,1024]{1,0:T(8,128)(2,1)S(1)} %copy-done.5, bf16[8,64,1024]{2,1,0:T(8,128)(2,1)S(1)} %copy-done, ...), custom_call_target="tpu_custom_call" | custom-call | tf_op jit(solution)/shard_map/pallas_call | solution.py:346
  33.8 0.6 %copy.14 = bf16[8,1024]{1,0:T(8,128)(2,1)} copy(bf16[8,1024]{1,0:T(8,128)(2,1)S(1)} %shard_map.118) | data formatting | bytes 32768
Async XLA Ops:
  0.0 1.2 %copy-start = (bf16[8,64,1024]{2,1,0:T(8,128)(2,1)S(1)}, bf16[8,64,1024]{2,1,0:T(8,128)(2,1)}, u32[]{:S(2)}) copy-start(bf16[8,64,1024]{2,1,0:T(8,128)(2,1)} %k_hbm.1) | copy-start | bytes 3145732
  1.2 1.2 %copy-start.1 = (bf16[8,64,1024]{2,1,0:T(8,128)(2,1)S(1)}, bf16[8,64,1024]{2,1,0:T(8,128)(2,1)}, u32[]{:S(2)}) copy-start(bf16[8,64,1024]{2,1,0:T(8,128)(2,1)} %v_hbm.1) | copy-start | bytes 3145732
  2.5 0.8 %copy-start.2 = (bf16[8,2048]{1,0:T(8,128)(2,1)S(1)}, bf16[8,2048]{1,0:T(8,128)(2,1)}, u32[]{:S(2)}) copy-start(bf16[8,2048]{1,0:T(8,128)(2,1)} %resid_hbm.1) | copy-start | bytes 98308
  3.2 0.7 %copy-start.3 = (bf16[8,1024]{1,0:T(8,128)(2,1)S(1)}, bf16[8,1024]{1,0:T(8,128)(2,1)}, u32[]{:S(2)}) copy-start(bf16[8,1024]{1,0:T(8,128)(2,1)} %q_hbm.1) | copy-start | bytes 49156
  3.9 0.7 %copy-start.4 = (bf16[8,1024]{1,0:T(8,128)(2,1)S(1)}, bf16[8,1024]{1,0:T(8,128)(2,1)}, u32[]{:S(2)}) copy-start(bf16[8,1024]{1,0:T(8,128)(2,1)} %nk_hbm.1) | copy-start | bytes 49156
  4.6 0.7 %copy-start.5 = (bf16[8,1024]{1,0:T(8,128)(2,1)S(1)}, bf16[8,1024]{1,0:T(8,128)(2,1)}, u32[]{:S(2)}) copy-start(bf16[8,1024]{1,0:T(8,128)(2,1)} %nv_hbm.1) | copy-start | bytes 49156
  5.4 0.7 %copy-start.6 = (f32[2048]{0:T(1024)S(1)}, f32[2048]{0:T(1024)}, u32[]{:S(2)}) copy-start(f32[2048]{0:T(1024)} %param.19) | copy-start | bytes 24580
  6.1 0.7 %copy-start.7 = (s32[8]{0:T(128)S(1)}, s32[8]{0:T(128)}, u32[]{:S(2)}) copy-start(s32[8]{0:T(128)} %lengths.1) | copy-start | bytes 100
  6.7 0.7 %copy-start.8 = (s32[8,1]{0,1:T(1,128)S(1)}, s32[8,1]{0,1:T(1,128)}, u32[]{:S(2)}) copy-start(s32[8,1]{0,1:T(1,128)} %param.21) | copy-start | bytes 100

commit v2 on v1

--- a/solution.py
+++ b/solution.py
@@ -38,8 +38,8 @@
 def kernel(
     n_data,
     n_cuts,
-    lengths,
-    experts,
+    lengths_hbm,
+    experts_hbm,
     q_hbm,
     nk_hbm,
     nv_hbm,
@@ -51,6 +51,8 @@
     wup_hbm,
     wdown_hbm,
     out_ref,
+    lengths,
+    experts,
     q_ref,
     nk_ref,
     nv_ref,
@@ -78,6 +80,8 @@
     z_recv,
     spread_send,
     spread_recv,
+    cross_send,
+    cross_recv,
     half_send,
     half_recv,
     red_send,
@@ -112,11 +116,13 @@
                 (wout_hbm, wout_ref),
                 (wup_hbm.at[0], wup_ref),
                 (wdown_hbm.at[0], wdown_ref),
+                (lengths_hbm, lengths),
+                (experts_hbm, experts),
             )
         )
     ]
-    for load in loads:
-        load.start()
+    for i in (0, 2, 1, 10, 4, 3, 11, 5, 6):
+        loads[i].start()
 
     cut_peers = [lax.rem(cut + d, n_cuts) for d in range(1, n_cuts)]
     e_peers = [lax.rem(me + d, n_e) for d in range(1, n_e)]
@@ -146,6 +152,8 @@
     own_new = div(iota((pairs, count), 0), heads) == iota((pairs, count), 1)
     fresh = jnp.sum(jnp.where(own_new, fresh_all, 0.0), axis=1, keepdims=True) * scale
     loads[2].wait()
+    loads[7].start()
+    loads[10].wait()
     span = count * length
     keys = k_ref[...].reshape(span, feats)
     scores = lax.dot_general(q_wide, keys, nt, preferred_element_type=F32) * scale
@@ -165,6 +173,8 @@
     loads[3].wait()
     new_rows = mm(spread_rows, nv_ref[...])
     loads[4].wait()
+    loads[8].start()
+    loads[9].start()
     summed = mm(pcache, v_ref[...].reshape(span, feats)) + pnew * new_rows
     summed = jnp.where(own_head, summed, 0.0).astype(BF16)
     join_rows = one_hot(div(iota((count, pairs), 1), heads) == iota((count, pairs), 0))
@@ -178,6 +188,7 @@
         copy.start()
         sent.append(copy)
 
+    loads[11].wait()
     ids_of = [experts[t] for t in range(count)]
     place = []
     for t in range(count):
@@ -185,9 +196,9 @@
         for u in range(t):
             slot = slot + jnp.where(ids_of[u] == ids_of[t], 1, 0)
         place.append(ids_of[t] * slots + slot)
-    nk = TILE // slots
-    chunk = width_all // nk
-    table_shape = (n_e * TILE, nk * count)
+    nq = min(TILE // slots, width // 128)
+    piece = width // nq
+    table_shape = (n_e * TILE, nq * count)
     row, col = iota(table_shape, 0), iota(table_shape, 1)
     target = jnp.zeros(table_shape, jnp.int32)
     for t in range(count):
@@ -206,27 +217,28 @@
     hidden = resid_ref[...].astype(F32) + attn
     hid_ref[...] = hidden
     meansq = jnp.mean(hidden * hidden, axis=1, keepdims=True)
-    normed = hidden * lax.rsqrt(meansq + 1e-06) * gain_ref[...]
-    stacked = jnp.concatenate([normed[:, k * chunk : (k + 1) * chunk] for k in range(nk)], axis=0)
+    own = pl.ds(pl.multiple_of(cut * width, width), width)
+    normed = hid_ref[:, own] * lax.rsqrt(meansq + 1e-06) * gain_ref[:, own]
+    stacked = jnp.concatenate([normed[:, k * piece : (k + 1) * piece] for k in range(nq)], axis=0)
     rows = mm(pack, stacked.astype(BF16)).astype(BF16)
-    packed[...] = rows.reshape(n_e, TILE, chunk)
+    packed[...] = rows.reshape(n_e, TILE, piece)
 
     for i, e in enumerate(e_peers):
         copy = remote(
-            packed.at[e], gath.at[g, me], z_send.at[i], z_recv.at[me], (e * GROUP + g, cut)
+            packed.at[e], gath.at[cut, g, me], z_send.at[i], z_recv.at[me], (e * GROUP + g, cut)
         )
         copy.start()
         sent.append(copy)
-    gath[g, me] = packed[me]
+    gath[cut, g, me] = packed[me]
     for i, e in enumerate([me] + e_peers):
         if i > 0:
             remote(
-                packed.at[e], gath.at[g, e], z_send.at[i - 1], z_recv.at[e], (e * GROUP + g, cut)
+                packed.at[e], gath.at[cut, g, e], z_send.at[0], z_recv.at[e], (e * GROUP + g, cut)
             ).wait_recv()
         for j, h in enumerate(g_peers):
             copy = remote(
-                gath.at[g, e],
-                gath.at[g, e],
+                gath.at[cut, g, e],
+                gath.at[cut, g, e],
                 spread_send.at[j, i],
                 spread_recv.at[g, e],
                 (me * GROUP + h, cut),
@@ -236,25 +248,38 @@
     all_rows = GROUP * n_e * slots
     per_group = n_e * slots
     wide = GROUP * n_e * TILE
-    row, col = iota((nk * all_rows, wide), 0), iota((nk * all_rows, wide), 1)
+    row, col = iota((nq * all_rows, wide), 0), iota((nq * all_rows, wide), 1)
     which, m = div(row, all_rows), mod(row, all_rows)
     unpack = one_hot(col == div(m, slots) * TILE + which * slots + mod(m, slots))
-    for i, e in enumerate([me] + e_peers):
-        for j, h in enumerate(g_peers):
-            remote(
-                gath.at[h, e],
-                gath.at[h, e],
-                spread_send.at[j, i],
-                spread_recv.at[h, e],
-                (me * GROUP + h, cut),
-            ).wait_recv()
-    arrived = mm(unpack, gath[...].reshape(wide, chunk)).astype(BF16)
+    for j, h in enumerate([g] + g_peers):
+        if j > 0:
+            for i, e in enumerate([me] + e_peers):
+                remote(
+                    gath.at[cut, h, e],
+                    gath.at[cut, h, e],
+                    spread_send.at[0, 0],
+                    spread_recv.at[h, e],
+                    (me * GROUP + h, cut),
+                ).wait_recv()
+        for i, c in enumerate(cut_peers):
+            copy = remote(
+                gath.at[cut, h], gath.at[cut, h], cross_send.at[i, j], cross_recv.at[cut, h], (dp, c)
+            )
+            copy.start()
+            sent.append(copy)
+
     loads[8].wait()
-    up = mm(arrived[0:all_rows], wup_ref[0:chunk, :])
-    for k in range(1, nk):
-        up = up + mm(
-            arrived[k * all_rows : (k + 1) * all_rows], wup_ref[k * chunk : (k + 1) * chunk, :]
-        )
+    up = jnp.zeros((all_rows, wup_ref.shape[1]), F32)
+    for i, c in enumerate([cut] + cut_peers):
+        if i > 0:
+            for h in range(GROUP):
+                remote(
+                    gath.at[c, h], gath.at[c, h], cross_send.at[0, 0], cross_recv.at[c, h], (dp, c)
+                ).wait_recv()
+        arrived = mm(unpack, gath[c].reshape(wide, piece)).astype(BF16)
+        for k in range(nq):
+            depth = pl.ds(pl.multiple_of(c * width + k * piece, piece), piece)
+            up = up + mm(arrived[k * all_rows : (k + 1) * all_rows], wup_ref[depth, :])
     act = jax.nn.gelu(up).astype(BF16)
 
     loads[9].wait()
@@ -275,8 +300,6 @@
         copy = remote(share.at[h], red.at[g], red_send.at[j], red_recv.at[g], (me * GROUP + h, cut))
         copy.start()
         sent.append(copy)
-    nq = min(TILE // slots, width // 128)
-    piece = width // nq
     row, col = iota((n_e * TILE, nq * per_group), 0), iota((n_e * TILE, nq * per_group), 1)
     repack = one_hot(
         (div(mod(row, TILE), slots) == div(col, per_group))
@@ -309,8 +332,7 @@
         ).wait_recv()
     returned = back[...].reshape(n_e * TILE, piece)
     expert_cols = jnp.concatenate([mm(pick, returned) for pick in picks], axis=1)
-    hidden_cols = hid_ref[:, pl.ds(pl.multiple_of(cut * width, width), width)]
-    out_ref[...] = (hidden_cols + expert_cols).astype(BF16)
+    out_ref[...] = (hid_ref[:, own] + expert_cols).astype(BF16)
     for copy in sent:
         copy.wait_send()
 
@@ -336,19 +358,19 @@
     width = width_all // n_cuts
     n_e = n_data // GROUP
     slots = max(2, 2 * count * GROUP // n_data)
-    chunk = width_all * slots // TILE
     piece = width // min(TILE // slots, width // 128)
     per_group = n_e * slots
     all_rows = GROUP * per_group
     dma = pltpu.SemaphoreType.DMA
-    smem = pl.BlockSpec(memory_space=pltpu.SMEM)
-    hbm = pl.BlockSpec(memory_space=pl.ANY)
+    hbm = pl.BlockSpec(memory_space=pltpu.HBM)
     return pl.pallas_call(
         functools.partial(kernel, n_data, n_cuts),
         out_shape=jax.ShapeDtypeStruct((count, width), BF16),
-        in_specs=[smem, smem] + [hbm] * 10,
+        in_specs=[hbm] * 12,
         out_specs=pl.BlockSpec(memory_space=pltpu.VMEM),
         scratch_shapes=[
+            pltpu.SMEM((count,), jnp.int32),
+            pltpu.SMEM((count,), jnp.int32),
             pltpu.VMEM(queries.shape, BF16),
             pltpu.VMEM(new_keys.shape, BF16),
             pltpu.VMEM(new_values.shape, BF16),
@@ -361,21 +383,23 @@
             pltpu.VMEM(w_down.shape[1:], BF16),
             pltpu.VMEM((n_cuts, count, width_all), F32),
             pltpu.VMEM((count, width_all), F32),
-            pltpu.VMEM((n_e, TILE, chunk), BF16),
-            pltpu.VMEM((GROUP, n_e, TILE, chunk), BF16),
+            pltpu.VMEM((n_e, TILE, piece), BF16),
+            pltpu.VMEM((n_cuts, GROUP, n_e, TILE, piece), BF16),
             pltpu.VMEM((n_cuts, all_rows, width), BF16),
             pltpu.VMEM((n_cuts, all_rows, width), BF16),
             pltpu.VMEM((GROUP, per_group, width), BF16),
             pltpu.VMEM((GROUP, per_group, width), BF16),
             pltpu.VMEM((n_e, TILE, piece), BF16),
             pltpu.VMEM((n_e, TILE, piece), BF16),
-            dma((10,)),
+            dma((12,)),
             dma((n_cuts,)),
             dma((n_cuts,)),
             dma((n_e,)),
             dma((n_e,)),
             dma((GROUP, n_e)),
             dma((GROUP, n_e)),
+            dma((n_cuts, GROUP)),
+            dma((n_cuts, GROUP)),
             dma((n_cuts,)),
             dma((n_cuts,)),
             dma((GROUP,)),
@@ -384,7 +408,7 @@
             dma((n_e,)),
         ],
         compiler_params=pltpu.CompilerParams(
-            collective_id=0, has_side_effects=True, vmem_limit_bytes=48 * 1024 * 1024
+            collective_id=0, has_side_effects=True, vmem_limit_bytes=60 * 1024 * 1024
         ),
     )(
         lengths,

time: 34.9 us -> 28.7 us (0.82)
  local copies, waits for them, and re-layouts: 7.97 us -> 1.32 us
  Pallas kernels: 26.4 us -> 27 us
    unnamed x19 -> x1, local copies, waits for them, and re-layouts: 7.97 us -> 1.32 us
    pallas_call x1, Pallas kernels: 26.4 us -> 27 us  [on_device(): pl.pallas_call(functools.partial(kernel, n_data, n_cuts), out_shape=jax.S...]
where the time goes in v2:
time: 28.7 us; the launch traced here: 28.4 us
  Pallas kernels  27 us (94%)
  local copies, waits for them, and re-layouts  1.32 us (5%)
    pallas_call x1, Pallas kernels, on_device(): pl.pallas_call(functools.partial(kernel, n_data, n_cuts), out_shape=jax.S...  27 us
    unnamed x1, local copies, waits for them, and re-layouts  1.32 us

profile of v2, /device:TPU:0, one launch (start us, length us, event | category | flops | bytes accessed | tf_op | source)
XLA Modules:
  0.0 28.4 jit_solution(17783238295627615576)
XLA Ops:
  0.0 27.0 %shard_map.118 = bf16[8,1024]{1,0:T(8,128)(2,1)} custom-call(s32[8]{0:T(128)} %lengths_hbm.1, s32[8]{0:T(128)} %bitcast.3, bf16[8,1024]{1,0:T(8,128)(2,1)} %q_hbm.1, bf16[8,1024]{1,0:T(8,128)(2,1)} %nk_hbm.1, bf16[8,1024]{1,0:T(8,128)(2,1)} %nv_hbm.1, bf16[8,64,1024]{2,1,0:T(8,128)(2,1)} %k_hbm.1, bf16[8,64,1024]{2,1,0:T(8,128)(2,1)} %v_hbm.1, ...), custom_call_target="tpu_custom_call" | custom-call | tf_op jit(solution)/shard_map/pallas_call | solution.py:366
  27.0 1.3 %copy.14 = bf16[8,1024]{1,0:T(8,128)(2,1)} copy(bf16[8,1024]{1,0:T(8,128)(2,1)} %shard_map.118) | data formatting | bytes 32768

commit v3 on v2

--- a/solution.py
+++ b/solution.py
@@ -121,7 +121,7 @@
             )
         )
     ]
-    for i in (0, 2, 1, 10, 4, 3, 11, 5, 6):
+    for i in (0, 10, 2, 1, 4, 3, 11, 5, 6):
         loads[i].start()
 
     cut_peers = [lax.rem(cut + d, n_cuts) for d in range(1, n_cuts)]
@@ -151,18 +151,18 @@
     fresh_all = lax.dot_general(q_wide, nk_ref[...], nt, preferred_element_type=F32)
     own_new = div(iota((pairs, count), 0), heads) == iota((pairs, count), 1)
     fresh = jnp.sum(jnp.where(own_new, fresh_all, 0.0), axis=1, keepdims=True) * scale
-    loads[2].wait()
-    loads[7].start()
     loads[10].wait()
     span = count * length
-    keys = k_ref[...].reshape(span, feats)
-    scores = lax.dot_general(q_wide, keys, nt, preferred_element_type=F32) * scale
     col = iota((1, span), 1)
     limit = jnp.zeros((1, span), jnp.int32)
     for t in range(count):
         limit = jnp.where(div(col, length) == t, lengths[t], limit)
     valid = jnp.where(mod(col, length) < limit, div(col, length), -1)
     keep = div(iota((pairs, span), 0), heads) == valid
+    loads[2].wait()
+    loads[7].start()
+    keys = k_ref[...].reshape(span, feats)
+    scores = lax.dot_general(q_wide, keys, nt, preferred_element_type=F32) * scale
     scores = jnp.where(keep, scores, -1e30)
     peak = jnp.maximum(jnp.max(scores, axis=1, keepdims=True), fresh)
     pcache = jnp.where(keep, jnp.exp(scores - peak), 0.0)
@@ -230,21 +230,16 @@
         copy.start()
         sent.append(copy)
     gath[cut, g, me] = packed[me]
-    for i, e in enumerate([me] + e_peers):
-        if i > 0:
-            remote(
-                packed.at[e], gath.at[cut, g, e], z_send.at[0], z_recv.at[e], (e * GROUP + g, cut)
-            ).wait_recv()
-        for j, h in enumerate(g_peers):
-            copy = remote(
-                gath.at[cut, g, e],
-                gath.at[cut, g, e],
-                spread_send.at[j, i],
-                spread_recv.at[g, e],
-                (me * GROUP + h, cut),
-            )
-            copy.start()
-            sent.append(copy)
+    for e in e_peers:
+        remote(
+            packed.at[e], gath.at[cut, g, e], z_send.at[0], z_recv.at[e], (e * GROUP + g, cut)
+        ).wait_recv()
+    for j, h in enumerate(g_peers):
+        copy = remote(
+            gath.at[cut, g], gath.at[cut, g], spread_send.at[j], spread_recv.at[g], (me * GROUP + h, cut)
+        )
+        copy.start()
+        sent.append(copy)
     all_rows = GROUP * n_e * slots
     per_group = n_e * slots
     wide = GROUP * n_e * TILE
@@ -253,14 +248,9 @@
     unpack = one_hot(col == div(m, slots) * TILE + which * slots + mod(m, slots))
     for j, h in enumerate([g] + g_peers):
         if j > 0:
-            for i, e in enumerate([me] + e_peers):
-                remote(
-                    gath.at[cut, h, e],
-                    gath.at[cut, h, e],
-                    spread_send.at[0, 0],
-                    spread_recv.at[h, e],
-                    (me * GROUP + h, cut),
-                ).wait_recv()
+            remote(
+                gath.at[cut, h], gath.at[cut, h], spread_send.at[0], spread_recv.at[h], (me * GROUP + h, cut)
+            ).wait_recv()
         for i, c in enumerate(cut_peers):
             copy = remote(
                 gath.at[cut, h], gath.at[cut, h], cross_send.at[i, j], cross_recv.at[cut, h], (dp, c)
@@ -269,7 +259,7 @@
             sent.append(copy)
 
     loads[8].wait()
-    up = jnp.zeros((all_rows, wup_ref.shape[1]), F32)
+    up = None
     for i, c in enumerate([cut] + cut_peers):
         if i > 0:
             for h in range(GROUP):
@@ -277,38 +267,57 @@
                     gath.at[c, h], gath.at[c, h], cross_send.at[0, 0], cross_recv.at[c, h], (dp, c)
                 ).wait_recv()
         arrived = mm(unpack, gath[c].reshape(wide, piece)).astype(BF16)
-        for k in range(nq):
-            depth = pl.ds(pl.multiple_of(c * width + k * piece, piece), piece)
-            up = up + mm(arrived[k * all_rows : (k + 1) * all_rows], wup_ref[depth, :])
+        arrived = jnp.concatenate(
+            [arrived[k * all_rows : (k + 1) * all_rows] for k in range(nq)], axis=1
+        )
+        term = mm(arrived, wup_ref[pl.ds(pl.multiple_of(c * width, width), width), :])
+        up = term if up is None else up + term
     act = jax.nn.gelu(up).astype(BF16)
 
     loads[9].wait()
-    for i, c in enumerate(cut_peers + [cut]):
-        columns = pl.ds(pl.multiple_of(c * width, width), width)
-        mine[c] = mm(act, wdown_ref[:, columns]).astype(BF16)
-        if i < n_cuts - 1:
-            copy = remote(mine.at[c], halves.at[cut], half_send.at[i], half_recv.at[cut], (dp, c))
+    runs, run = share.shape[0], share.shape[3]
+
+    def down(c, r):
+        columns = pl.ds(pl.multiple_of(c * width + r * run, run), run)
+        return mm(act, wdown_ref[:, columns]).astype(BF16)
+
+    for i, c in enumerate(cut_peers):
+        for r in range(runs):
+            mine[c, r] = down(c, r)
+            copy = remote(
+                mine.at[c, r], halves.at[cut, r], half_send.at[i, r], half_recv.at[cut, r], (dp, c)
+            )
             copy.start()
             sent.append(copy)
-    summed = mine[cut].astype(F32)
-    for i, c in enumerate(cut_peers):
-        remote(mine.at[c], halves.at[c], half_send.at[i], half_recv.at[c], (dp, c)).wait_recv()
-        summed = summed + halves[c].astype(F32)
-    share[...] = summed.astype(BF16).reshape(GROUP, per_group, width)
-
-    for j, h in enumerate(g_peers):
-        copy = remote(share.at[h], red.at[g], red_send.at[j], red_recv.at[g], (me * GROUP + h, cut))
-        copy.start()
-        sent.append(copy)
+    for r in range(runs):
+        summed = down(cut, r).astype(F32)
+        for c in cut_peers:
+            remote(
+                mine.at[c, r], halves.at[c, r], half_send.at[0, r], half_recv.at[c, r], (dp, c)
+            ).wait_recv()
+            summed = summed + halves[c, r].astype(F32)
+        share[r] = summed.astype(BF16).reshape(GROUP, per_group, run)
+        for j, h in enumerate(g_peers):
+            copy = remote(
+                share.at[r, h], red.at[r, g], red_send.at[r, j], red_recv.at[r, g], (me * GROUP + h, cut)
+            )
+            copy.start()
+            sent.append(copy)
     row, col = iota((n_e * TILE, nq * per_group), 0), iota((n_e * TILE, nq * per_group), 1)
     repack = one_hot(
         (div(mod(row, TILE), slots) == div(col, per_group))
         & (div(row, TILE) * slots + mod(row, slots) == mod(col, per_group))
     )
-    summed = share[g].astype(F32)
-    for j, h in enumerate(g_peers):
-        remote(share.at[h], red.at[h], red_send.at[j], red_recv.at[h], (me * GROUP + h, cut)).wait_recv()
-        summed = summed + red[h].astype(F32)
+    totals = []
+    for r in range(runs):
+        summed = share[r, g].astype(F32)
+        for h in g_peers:
+            remote(
+                share.at[r, h], red.at[r, h], red_send.at[r, 0], red_recv.at[r, h], (me * GROUP + h, cut)
+            ).wait_recv()
+            summed = summed + red[r, h].astype(F32)
+        totals.append(summed)
+    summed = jnp.concatenate(totals, axis=1)
     stacked = jnp.concatenate([summed[:, k * piece : (k + 1) * piece] for k in range(nq)], axis=0)
     going[...] = mm(repack, stacked.astype(BF16)).astype(BF16).reshape(n_e, TILE, piece)
 
@@ -326,6 +335,8 @@
         target = jnp.where(row == t, place[t], target)
     found = div(col, TILE) * slots + mod(col, slots) == target
     picks = [one_hot(found & (div(mod(col, TILE), slots) == k)) for k in range(nq)]
+    for copy in sent:
+        copy.wait_send()
     for i, e in enumerate(e_peers):
         remote(
             going.at[e], back.at[e], back_send.at[i], back_recv.at[e], (e * GROUP + g, cut)
@@ -333,8 +344,6 @@
     returned = back[...].reshape(n_e * TILE, piece)
     expert_cols = jnp.concatenate([mm(pick, returned) for pick in picks], axis=1)
     out_ref[...] = (hid_ref[:, own] + expert_cols).astype(BF16)
-    for copy in sent:
-        copy.wait_send()
 
 
 def on_device(
@@ -361,11 +370,13 @@
     piece = width // min(TILE // slots, width // 128)
     per_group = n_e * slots
     all_rows = GROUP * per_group
+    runs = 2 if width % 256 == 0 else 1
+    run = width // runs
     dma = pltpu.SemaphoreType.DMA
     hbm = pl.BlockSpec(memory_space=pltpu.HBM)
     return pl.pallas_call(
         functools.partial(kernel, n_data, n_cuts),
-        out_shape=jax.ShapeDtypeStruct((count, width), BF16),
+        out_shape=pltpu.VMEM((count, width), BF16),
         in_specs=[hbm] * 12,
         out_specs=pl.BlockSpec(memory_space=pltpu.VMEM),
         scratch_shapes=[
@@ -385,10 +396,10 @@
             pltpu.VMEM((count, width_all), F32),
             pltpu.VMEM((n_e, TILE, piece), BF16),
             pltpu.VMEM((n_cuts, GROUP, n_e, TILE, piece), BF16),
-            pltpu.VMEM((n_cuts, all_rows, width), BF16),
-            pltpu.VMEM((n_cuts, all_rows, width), BF16),
-            pltpu.VMEM((GROUP, per_group, width), BF16),
-            pltpu.VMEM((GROUP, per_group, width), BF16),
+            pltpu.VMEM((n_cuts, runs, all_rows, run), BF16),
+            pltpu.VMEM((n_cuts, runs, all_rows, run), BF16),
+            pltpu.VMEM((runs, GROUP, per_group, run), BF16),
+            pltpu.VMEM((runs, GROUP, per_group, run), BF16),
             pltpu.VMEM((n_e, TILE, piece), BF16),
             pltpu.VMEM((n_e, TILE, piece), BF16),
             dma((12,)),
@@ -396,14 +407,14 @@
             dma((n_cuts,)),
             dma((n_e,)),
             dma((n_e,)),
-            dma((GROUP, n_e)),
-            dma((GROUP, n_e)),
+            dma((GROUP,)),
+            dma((GROUP,)),
             dma((n_cuts, GROUP)),
             dma((n_cuts, GROUP)),
-            dma((n_cuts,)),
-            dma((n_cuts,)),
-            dma((GROUP,)),
-            dma((GROUP,)),
+            dma((n_cuts, runs)),
+            dma((n_cuts, runs)),
+            dma((runs, GROUP)),
+            dma((runs, GROUP)),
             dma((n_e,)),
             dma((n_e,)),
         ],

time: 28.7 us -> 27.3 us (0.951)
  local copies, waits for them, and re-layouts: 1.32 us -> 0.61 us
  Pallas kernels: 27 us -> 26.5 us
    unnamed x1, local copies, waits for them, and re-layouts: 1.32 us -> 0.61 us
    pallas_call x1, Pallas kernels: 27 us -> 26.5 us  [on_device(): pl.pallas_call(functools.partial(kernel, n_data, n_cuts), out_shape=pltpu...]
where the time goes in v3:
time: 27.3 us; the launch traced here: 27.1 us
  Pallas kernels  26.5 us (97%)
  local copies, waits for them, and re-layouts  0.61 us (2%)
    pallas_call x1, Pallas kernels, on_device(): pl.pallas_call(functools.partial(kernel, n_data, n_cuts), out_shape=pltpu...  26.5 us
    unnamed x1, local copies, waits for them, and re-layouts  0.61 us

profile of v3, /device:TPU:0, one launch (start us, length us, event | category | flops | bytes accessed | tf_op | source)
XLA Modules:
  0.0 27.1 jit_solution(12522441922365381327)
XLA Ops:
  0.0 26.5 %shard_map.118 = bf16[8,1024]{1,0:T(8,128)(2,1)S(1)} custom-call(s32[8]{0:T(128)} %lengths_hbm.1, s32[8]{0:T(128)} %bitcast.3, bf16[8,1024]{1,0:T(8,128)(2,1)} %q_hbm.1, bf16[8,1024]{1,0:T(8,128)(2,1)} %nk_hbm.1, bf16[8,1024]{1,0:T(8,128)(2,1)} %nv_hbm.1, bf16[8,64,1024]{2,1,0:T(8,128)(2,1)} %k_hbm.1, bf16[8,64,1024]{2,1,0:T(8,128)(2,1)} %v_hbm.1, ...), custom_call_target="tpu_custom_call" | custom-call | tf_op jit(solution)/shard_map/pallas_call | solution.py:377
  26.5 0.6 %copy.14 = bf16[8,1024]{1,0:T(8,128)(2,1)} copy(bf16[8,1024]{1,0:T(8,128)(2,1)S(1)} %shard_map.118) | data formatting | bytes 32768

commit v4 on v3

--- a/solution.py
+++ b/solution.py
@@ -102,27 +102,37 @@
     slots = max(2, 2 * count * GROUP // n_data)
     scale = 1.0 / HD**0.5
 
+    def pieces(src, dst, n, first):
+        size = dst.shape[0] // n
+        return [
+            pltpu.make_async_copy(
+                src.at[pl.ds(i * size, size)], dst.at[pl.ds(i * size, size)], load_sem.at[first + i]
+            )
+            for i in range(n)
+        ]
+
+    n_out = min(4, feats // 128)
     loads = [
         pltpu.make_async_copy(src, dst, load_sem.at[i])
         for i, (src, dst) in enumerate(
             (
                 (q_hbm, q_ref),
+                (lengths_hbm, lengths),
                 (nk_hbm, nk_ref),
-                (k_hbm, k_ref),
                 (nv_hbm, nv_ref),
-                (v_hbm, v_ref),
+                (experts_hbm, experts),
                 (resid_hbm, resid_ref),
                 (gain_hbm, gain_ref),
-                (wout_hbm, wout_ref),
-                (wup_hbm.at[0], wup_ref),
-                (wdown_hbm.at[0], wdown_ref),
-                (lengths_hbm, lengths),
-                (experts_hbm, experts),
             )
         )
     ]
-    for i in (0, 10, 2, 1, 4, 3, 11, 5, 6):
-        loads[i].start()
+    load_keys = pieces(k_hbm, k_ref, 2, 7)
+    load_values = pieces(v_hbm, v_ref, 2, 9)
+    load_out = pieces(wout_hbm, wout_ref, n_out, 11)
+    load_up = pieces(wup_hbm.at[0], wup_ref, 4, 15)
+    load_down = pieces(wdown_hbm.at[0], wdown_ref, 4, 19)
+    for load in loads[:2] + load_keys + loads[2:3] + load_values + loads[3:]:
+        load.start()
 
     cut_peers = [lax.rem(cut + d, n_cuts) for d in range(1, n_cuts)]
     e_peers = [lax.rem(me + d, n_e) for d in range(1, n_e)]
@@ -145,13 +155,15 @@
     spread_rows = one_hot(div(iota((pairs, count), 0), heads) == iota((pairs, count), 1))
     own_head = div(iota((pairs, feats), 1), HD) == mod(iota((pairs, feats), 0), heads)
     loads[0].wait()
+    for load in load_out:
+        load.start()
     q_wide = jnp.where(own_head, mm(spread_rows, q_ref[...]), 0.0).astype(BF16)
     nt = (((1,), (1,)), ((), ()))
-    loads[1].wait()
+    loads[2].wait()
     fresh_all = lax.dot_general(q_wide, nk_ref[...], nt, preferred_element_type=F32)
     own_new = div(iota((pairs, count), 0), heads) == iota((pairs, count), 1)
     fresh = jnp.sum(jnp.where(own_new, fresh_all, 0.0), axis=1, keepdims=True) * scale
-    loads[10].wait()
+    loads[1].wait()
     span = count * length
     col = iota((1, span), 1)
     limit = jnp.zeros((1, span), jnp.int32)
@@ -159,8 +171,8 @@
         limit = jnp.where(div(col, length) == t, lengths[t], limit)
     valid = jnp.where(mod(col, length) < limit, div(col, length), -1)
     keep = div(iota((pairs, span), 0), heads) == valid
-    loads[2].wait()
-    loads[7].start()
+    for load in load_keys:
+        load.wait()
     keys = k_ref[...].reshape(span, feats)
     scores = lax.dot_general(q_wide, keys, nt, preferred_element_type=F32) * scale
     scores = jnp.where(keep, scores, -1e30)
@@ -172,23 +184,30 @@
     pnew = (pnew / total).astype(BF16).astype(F32)
     loads[3].wait()
     new_rows = mm(spread_rows, nv_ref[...])
-    loads[4].wait()
-    loads[8].start()
-    loads[9].start()
+    for load in load_values:
+        load.wait()
     summed = mm(pcache, v_ref[...].reshape(span, feats)) + pnew * new_rows
     summed = jnp.where(own_head, summed, 0.0).astype(BF16)
     join_rows = one_hot(div(iota((count, pairs), 1), heads) == iota((count, pairs), 0))
     heads_out = mm(join_rows, summed).astype(BF16)
 
-    loads[7].wait()
-    parts[cut] = mm(heads_out, wout_ref[...])
+    depth = feats // n_out
+    partial = jnp.zeros((count, width_all), F32)
+    for i, load in enumerate(load_out):
+        load.wait()
+        if i == n_out - 1:
+            for later in load_up + load_down:
+                later.start()
+        block = slice(i * depth, (i + 1) * depth)
+        partial = partial + mm(heads_out[:, block], wout_ref[block, :])
+    parts[cut] = partial
     pl.semaphore_wait(barrier, len(ids))
     for i, c in enumerate(cut_peers):
         copy = remote(parts.at[cut], parts.at[cut], part_send.at[i], part_recv.at[cut], (dp, c))
         copy.start()
         sent.append(copy)
 
-    loads[11].wait()
+    loads[4].wait()
     ids_of = [experts[t] for t in range(count)]
     place = []
     for t in range(count):
@@ -258,7 +277,8 @@
             copy.start()
             sent.append(copy)
 
-    loads[8].wait()
+    for load in load_up:
+        load.wait()
     up = None
     for i, c in enumerate([cut] + cut_peers):
         if i > 0:
@@ -274,7 +294,8 @@
         up = term if up is None else up + term
     act = jax.nn.gelu(up).astype(BF16)
 
-    loads[9].wait()
+    for load in load_down:
+        load.wait()
     runs, run = share.shape[0], share.shape[3]
 
     def down(c, r):
@@ -402,7 +423,7 @@
             pltpu.VMEM((runs, GROUP, per_group, run), BF16),
             pltpu.VMEM((n_e, TILE, piece), BF16),
             pltpu.VMEM((n_e, TILE, piece), BF16),
-            dma((12,)),
+            dma((23,)),
             dma((n_cuts,)),
             dma((n_cuts,)),
             dma((n_e,)),

time: 27.3 us -> 26.5 us (0.971)
  Pallas kernels: 26.5 us -> 25.6 us
    pallas_call x1, Pallas kernels: 26.5 us -> 25.6 us  [on_device(): pl.pallas_call(functools.partial(kernel, n_data, n_cuts), out_shape=pltpu...]
where the time goes in v4:
time: 26.5 us; the launch traced here: 26.2 us
  Pallas kernels  25.6 us (97%)
  local copies, waits for them, and re-layouts  0.61 us (2%)
    pallas_call x1, Pallas kernels, on_device(): pl.pallas_call(functools.partial(kernel, n_data, n_cuts), out_shape=pltpu...  25.6 us
    unnamed x1, local copies, waits for them, and re-layouts  0.61 us

profile of v4, /device:TPU:0, one launch (start us, length us, event | category | flops | bytes accessed | tf_op | source)
XLA Modules:
  0.0 26.2 jit_solution(9616351141261079434)
XLA Ops:
  0.0 25.6 %shard_map.118 = bf16[8,1024]{1,0:T(8,128)(2,1)S(1)} custom-call(s32[8]{0:T(128)} %lengths_hbm.1, s32[8]{0:T(128)} %bitcast.3, bf16[8,1024]{1,0:T(8,128)(2,1)} %q_hbm.1, bf16[8,1024]{1,0:T(8,128)(2,1)} %nk_hbm.1, bf16[8,1024]{1,0:T(8,128)(2,1)} %nv_hbm.1, bf16[8,64,1024]{2,1,0:T(8,128)(2,1)} %k_hbm.1, bf16[8,64,1024]{2,1,0:T(8,128)(2,1)} %v_hbm.1, ...), custom_call_target="tpu_custom_call" | custom-call | tf_op jit(solution)/shard_map/pallas_call | solution.py:398
  25.6 0.6 %copy.14 = bf16[8,1024]{1,0:T(8,128)(2,1)} copy(bf16[8,1024]{1,0:T(8,128)(2,1)S(1)} %shard_map.118) | data formatting | bytes 32768

commit v5 on v4

--- a/solution.py
+++ b/solution.py
@@ -244,21 +244,33 @@
 
     for i, e in enumerate(e_peers):
         copy = remote(
-            packed.at[e], gath.at[cut, g, me], z_send.at[i], z_recv.at[me], (e * GROUP + g, cut)
+            packed.at[e],
+            gath.at[cut, g, n_e - 1 - i],
+            z_send.at[i],
+            z_recv.at[n_e - 1 - i],
+            (e * GROUP + g, cut),
         )
         copy.start()
         sent.append(copy)
-    gath[cut, g, me] = packed[me]
-    for e in e_peers:
-        remote(
-            packed.at[e], gath.at[cut, g, e], z_send.at[0], z_recv.at[e], (e * GROUP + g, cut)
-        ).wait_recv()
-    for j, h in enumerate(g_peers):
-        copy = remote(
-            gath.at[cut, g], gath.at[cut, g], spread_send.at[j], spread_recv.at[g], (me * GROUP + h, cut)
-        )
-        copy.start()
-        sent.append(copy)
+    gath[cut, g, 0] = packed[me]
+    spread = (pl.ds(0, 1), pl.ds(1, n_e - 1))
+    for part in range(2):
+        if part == 1:
+            for i, e in enumerate(e_peers):
+                remote(
+                    packed.at[e],
+                    gath.at[cut, g, i + 1],
+                    z_send.at[i],
+                    z_recv.at[i + 1],
+                    (e * GROUP + g, cut),
+                ).wait_recv()
+        block = gath.at[cut, g, spread[part]]
+        for j, h in enumerate(g_peers):
+            copy = remote(
+                block, block, spread_send.at[part, j], spread_recv.at[part, g], (me * GROUP + h, cut)
+            )
+            copy.start()
+            sent.append(copy)
     all_rows = GROUP * n_e * slots
     per_group = n_e * slots
     wide = GROUP * n_e * TILE
@@ -267,9 +279,11 @@
     unpack = one_hot(col == div(m, slots) * TILE + which * slots + mod(m, slots))
     for j, h in enumerate([g] + g_peers):
         if j > 0:
-            remote(
-                gath.at[cut, h], gath.at[cut, h], spread_send.at[0], spread_recv.at[h], (me * GROUP + h, cut)
-            ).wait_recv()
+            for part in range(2):
+                block = gath.at[cut, h, spread[part]]
+                remote(
+                    block, block, spread_send.at[part, 0], spread_recv.at[part, h], (me * GROUP + h, cut)
+                ).wait_recv()
         for i, c in enumerate(cut_peers):
             copy = remote(
                 gath.at[cut, h], gath.at[cut, h], cross_send.at[i, j], cross_recv.at[cut, h], (dp, c)
@@ -344,11 +358,11 @@
 
     for i, e in enumerate(e_peers):
         copy = remote(
-            going.at[e], back.at[me], back_send.at[i], back_recv.at[me], (e * GROUP + g, cut)
+            going.at[i + 1], back.at[me], back_send.at[i], back_recv.at[me], (e * GROUP + g, cut)
         )
         copy.start()
         sent.append(copy)
-    back[me] = going[me]
+    back[me] = going[0]
     table_shape = (count, n_e * TILE)
     row, col = iota(table_shape, 0), iota(table_shape, 1)
     target = jnp.zeros(table_shape, jnp.int32)
@@ -360,7 +374,7 @@
         copy.wait_send()
     for i, e in enumerate(e_peers):
         remote(
-            going.at[e], back.at[e], back_send.at[i], back_recv.at[e], (e * GROUP + g, cut)
+            going.at[i + 1], back.at[e], back_send.at[i], back_recv.at[e], (e * GROUP + g, cut)
         ).wait_recv()
     returned = back[...].reshape(n_e * TILE, piece)
     expert_cols = jnp.concatenate([mm(pick, returned) for pick in picks], axis=1)
@@ -428,8 +442,8 @@
             dma((n_cuts,)),
             dma((n_e,)),
             dma((n_e,)),
-            dma((GROUP,)),
-            dma((GROUP,)),
+            dma((2, GROUP)),
+            dma((2, GROUP)),
             dma((n_cuts, GROUP)),
             dma((n_cuts, GROUP)),
             dma((n_cuts, runs)),

time: 26.5 us -> 26.2 us (0.989)
  no operation moved by 1% of the time
where the time goes in v5:
time: 26.2 us; the launch traced here: 26 us
  Pallas kernels  25.4 us (97%)
  local copies, waits for them, and re-layouts  0.61 us (2%)
    pallas_call x1, Pallas kernels, on_device(): pl.pallas_call(functools.partial(kernel, n_data, n_cuts), out_shape=pltpu...  25.4 us
    unnamed x1, local copies, waits for them, and re-layouts  0.61 us

profile of v5, /device:TPU:0, one launch (start us, length us, event | category | flops | bytes accessed | tf_op | source)
XLA Modules:
  0.0 26.0 jit_solution(17661793026485078265)
XLA Ops:
  0.0 25.4 %shard_map.118 = bf16[8,1024]{1,0:T(8,128)(2,1)S(1)} custom-call(s32[8]{0:T(128)} %lengths_hbm.1, s32[8]{0:T(128)} %bitcast.3, bf16[8,1024]{1,0:T(8,128)(2,1)} %q_hbm.1, bf16[8,1024]{1,0:T(8,128)(2,1)} %nk_hbm.1, bf16[8,1024]{1,0:T(8,128)(2,1)} %nv_hbm.1, bf16[8,64,1024]{2,1,0:T(8,128)(2,1)} %k_hbm.1, bf16[8,64,1024]{2,1,0:T(8,128)(2,1)} %v_hbm.1, ...), custom_call_target="tpu_custom_call" | custom-call | tf_op jit(solution)/shard_map/pallas_call | solution.py:412
  25.4 0.6 %copy.14 = bf16[8,1024]{1,0:T(8,128)(2,1)} copy(bf16[8,1024]{1,0:T(8,128)(2,1)S(1)} %shard_map.118) | data formatting | bytes 32768
